TPU v7x, 32 devices: a whole 2x2x4 slice. The times are simulated.
32 devices in a mesh: dp: 4 (over x, core), seq: 8 (over z, y).
Axes of the slice: x: 2, y: 2, z: 4, core: 2. Of those that a mesh axis runs over, the one named last changes fastest.
Arguments:
- signal: float32 [32, 512, 1024], P('seq', None, 'dp'), may hold values from -6 to 6
- gate: float32 [32, 512, 1024], P('seq', None, 'dp'), may hold values from -6 to 6
- cotangent: float32 [32, 512, 1024], P('seq', None, 'dp'), may hold values from -6 to 6
- kernel: float32 [2, 32, 512, 1024], P(None, 'seq', None, 'dp'), may hold values from -6 to 6
- out_weight: float32 [1024, 1024], P('dp'), may hold values from -0.1875 to 0.1875
Outputs:
- output: float32 [32, 512, 1024], P('seq', None, 'dp')
- gate_grad: float32 [32, 512, 1024], P('seq', None, 'dp')
- input_grad: float32 [32, 512, 1024], P('seq', None, 'dp')
- kernel_grad: float32 [2, 32, 512, 1024], P(None, 'seq', None, 'dp')
- weight_grad: float32 [1024, 1024], P('dp')
All inputs are finite; a program needn't handle non-finite values.
Results may differ from a plain program's by a relative error of at most 0.000098.
Values sent between devices are 32-bit elements; how exact they have to be, the bound alone decides.
A program may use at most 128 MiB of HBM per device.

v0:
```python
import math

import jax
import jax.numpy as jnp
from jax import lax
from jax.sharding import PartitionSpec as P

N1 = 32
N2 = 512


PRECISE = lax.Precision.HIGHEST


def angle_table(rows, cols, modulus):
    product = rows[:, None] * cols[None, :] % modulus
    return product.astype(jnp.float32) * (2.0 * math.pi / modulus)


def contract(form, matrix, field):
    return jnp.einsum(form, matrix, field, precision=PRECISE)


def forward(fields):
    planes = fields.shape[0]
    devices = lax.axis_size("seq")
    position = lax.axis_index("seq")
    block_cols = N2 // devices
    index_rows = jnp.arange(N1, dtype=jnp.int32)
    index_cols = jnp.arange(N2, dtype=jnp.int32)
    angle_rows = angle_table(index_rows, index_rows, N1)
    cosine_rows, sine_rows = (jnp.cos(angle_rows), jnp.sin(angle_rows))
    gathered = lax.all_to_all(fields, "seq", split_axis=2, concat_axis=1, tiled=True)
    real_part = contract("ka,pabc->pkbc", cosine_rows, gathered)
    imag_part = -contract("ka,pabc->pkbc", sine_rows, gathered)
    global_cols = position * block_cols + jnp.arange(block_cols, dtype=jnp.int32)
    twist = angle_table(index_rows, global_cols, N1 * N2)
    twist_cosine = jnp.cos(twist)[None, :, :, None]
    twist_sine = jnp.sin(twist)[None, :, :, None]
    turned_re = real_part * twist_cosine + imag_part * twist_sine
    turned_im = imag_part * twist_cosine - real_part * twist_sine
    stacked = jnp.concatenate([turned_re, turned_im], axis=0)
    moved = lax.all_to_all(stacked, "seq", split_axis=1, concat_axis=2, tiled=True)
    moved_re = moved[:planes]
    moved_im = moved[planes:]
    angle_cols = angle_table(index_cols, index_cols, N2)
    cosine_cols, sine_cols = (jnp.cos(angle_cols), jnp.sin(angle_cols))
    result_re = contract("mb,pkbc->pkmc", cosine_cols, moved_re) + contract(
        "mb,pkbc->pkmc", sine_cols, moved_im
    )
    result_im = contract("mb,pkbc->pkmc", cosine_cols, moved_im) - contract(
        "mb,pkbc->pkmc", sine_cols, moved_re
    )
    return (result_re, result_im)


def inverse(spec_re, spec_im):
    planes = spec_re.shape[0]
    devices = lax.axis_size("seq")
    position = lax.axis_index("seq")
    freq_rows = N1 // devices
    index_rows = jnp.arange(N1, dtype=jnp.int32)
    index_cols = jnp.arange(N2, dtype=jnp.int32)
    angle_cols = angle_table(index_cols, index_cols, N2)
    cosine_cols, sine_cols = (jnp.cos(angle_cols), jnp.sin(angle_cols))
    half_re = contract("bm,pkmc->pkbc", cosine_cols, spec_re) - contract(
        "bm,pkmc->pkbc", sine_cols, spec_im
    )
    half_im = contract("bm,pkmc->pkbc", cosine_cols, spec_im) + contract(
        "bm,pkmc->pkbc", sine_cols, spec_re
    )
    global_rows = position * freq_rows + jnp.arange(freq_rows, dtype=jnp.int32)
    twist = angle_table(global_rows, index_cols, N1 * N2)
    twist_cosine = jnp.cos(twist)[None, :, :, None]
    twist_sine = jnp.sin(twist)[None, :, :, None]
    turned_re = half_re * twist_cosine - half_im * twist_sine
    turned_im = half_im * twist_cosine + half_re * twist_sine
    stacked = jnp.concatenate([turned_re, turned_im], axis=0)
    moved = lax.all_to_all(stacked, "seq", split_axis=2, concat_axis=1, tiled=True)
    angle_rows = angle_table(index_rows, index_rows, N1)
    cosine_rows, sine_rows = (jnp.cos(angle_rows), jnp.sin(angle_rows))
    real_out = contract("ak,pkbc->pabc", cosine_rows, moved[:planes]) - contract(
        "ak,pkbc->pabc", sine_rows, moved[planes:]
    )
    real_out = real_out * (1.0 / (N1 * N2))
    return lax.all_to_all(real_out, "seq", split_axis=1, concat_axis=2, tiled=True)


def on_device(signal, gate, cotangent, kernel, out_weight):
    kern_re = kernel[0]
    kern_im = kernel[1]
    cot_full = lax.all_gather(cotangent, "dp", axis=2, tiled=True)
    gated_grad = jnp.einsum("abo,co->abc", cot_full, out_weight, precision=PRECISE)
    conv_grad = gated_grad * gate
    spec_re, spec_im = forward(signal[None])
    signal_re, signal_im = (spec_re[0], spec_im[0])
    mixed = inverse(
        (kern_re * signal_re - kern_im * signal_im)[None],
        (kern_re * signal_im + kern_im * signal_re)[None],
    )[0]
    back_re, back_im = forward(conv_grad[None])
    grad_re, grad_im = (back_re[0], back_im[0])
    input_grad = inverse(
        (kern_re * grad_re + kern_im * grad_im)[None], (kern_re * grad_im - kern_im * grad_re)[None]
    )[0]
    kernel_grad = jnp.stack(
        [signal_re * grad_re + signal_im * grad_im, signal_re * grad_im - signal_im * grad_re]
    ) * (1.0 / (N1 * N2))
    gated = gate * mixed
    gate_grad = gated_grad * mixed
    out_term = jnp.einsum("abc,co->abo", gated, out_weight, precision=PRECISE)
    output = lax.psum_scatter(out_term, "dp", scatter_dimension=2, tiled=True)
    weight_part = jnp.einsum("abc,abo->co", gated, cot_full, precision=PRECISE)
    weight_grad = lax.psum(weight_part, "seq")
    return (output, gate_grad, input_grad, kernel_grad, weight_grad)


def solution(mesh):
    placed = (
        P("seq", None, "dp"),
        P("seq", None, "dp"),
        P("seq", None, "dp"),
        P(None, "seq", None, "dp"),
        P("dp", None),
    )
    return jax.shard_map(
        on_device,
        mesh=mesh,
        in_specs=placed,
        out_specs=(
            P("seq", None, "dp"),
            P("seq", None, "dp"),
            P("seq", None, "dp"),
            P(None, "seq", None, "dp"),
            P("dp", None),
        ),
        check_vma=False,
    )
```

profile of v0, /device:TPU:0, one launch (start us, length us, event | category | flops | bytes accessed | tf_op | source)
XLA Modules:
  0.0 879.7 jit_solution(1940531042983054670)
XLA Ops:
  8.9 2.7 copy.132
  11.5 7.3 all-to-all-start
  18.8 51.8 %all-gather.2.cloned.1.call-done = f32[4,512,1024]{2,1,0:T(8,128)} async-done(((f32[4,512,256]{2,1,0:T(8,128)}), f32[4,512,1024]{2,1,0:T(8,128)}) %all-gather.2.cloned.1.call-update) | async-done | bytes 8388624 | tf_op jit(solution)/shard_map/all_gather | solution.py:92
  70.6 9.1 %fusion.43 = f32[4,512,256]{2,1,0:T(8,128)S(1)} fusion(f32[4,512,1024]{2,1,0:T(8,128)} %all-gather.2.cloned.1.call-done, f32[256,1024]{1,0:T(8,128)S(1)} %copy-done), kind=kOutput, calls=%fused_computation.82 | convolution fusion | flops 6442450944 | bytes 11534336 | tf_op jit(solution)/shard_map/abo,co->abc/dot_general | solution.py:93
  81.1 2.7 copy.98
  83.8 5.8 all-to-all-start.4
  89.8 3.5 copy.131
  95.3 3.3 fusion.107
  98.6 3.3 fusion.115
  101.8 36.4 %all-to-all-done.4 = f32[1,4,512,256]{3,1,0,2:T(4,128)} async-done(((f32[1,4,512,256]{3,1,0,2:T(4,128)}), f32[1,4,512,256]{3,1,0,2:T(4,128)}, u32[]{:S(2)}, u32[]{:S(2)}) %all-to-all-start.4) | async-done | bytes 2097184 | tf_op jit(solution)/shard_map/all_to_all | solution.py:33
  138.3 3.5 copy.130
  146.0 4.4 fusion.13
  150.7 4.4 copy.100
  155.2 4.7 all-to-all-start.5
  161.9 4.4 copy.83
  166.3 86.3 %all-to-all-done.5 = f32[2,32,64,256]{3,2,0,1:T(8,128)} async-done(((f32[2,32,64,256]{3,2,0,1:T(8,128)}), f32[2,32,64,256]{3,2,0,1:T(8,128)}, u32[]{:S(2)}, u32[]{:S(2)}) %all-to-all-start.5) | async-done | bytes 4194336 | tf_op jit(solution)/shard_map/all_to_all | solution.py:43
  252.7 4.6 all-to-all-start.1
  257.3 3.9 fusion.236
  261.2 3.3 copy.126
  266.5 2.5 copy.101
  269.8 10.9 %fusion.60 = f32[4,256,512]{2,1,0:T(8,128)S(1)} fusion(f32[4,512,256]{2,1,0:T(8,128)S(1)} %bitcast.317), kind=kOutput, calls=%fused_computation.99 | convolution fusion | flops 3224895488 | bytes 4194304 | tf_op jit(solution)/shard_map/mb,pkbc->pkmc/dot_general | solution.py:21
  280.7 11.1 %fusion.62 = f32[4,256,512]{2,1,0:T(8,128)S(1)} fusion(f32[4,512,256]{2,1,0:T(8,128)S(1)} %bitcast.319), kind=kOutput, calls=%fused_computation.101 | convolution fusion | flops 3224895488 | bytes 4194304 | tf_op jit(solution)/shard_map/mb,pkbc->pkmc/dot_general | solution.py:21
  291.8 11.2 %convolution_subtract_fusion = f32[4,256,512]{2,1,0:T(8,128)S(1)} fusion(f32[4,256,512]{2,1,0:T(8,128)S(1)} %fusion.60, f32[4,512,256]{2,1,0:T(8,128)S(1)} %bitcast.320), kind=kOutput, calls=%fused_computation.71 | convolution fusion | flops 3225419776 | bytes 6291456 | tf_op jit(solution)/shard_map/mb,pkbc->pkmc/dot_general | solution.py:21
  303.0 11.8 %convolution_add_fusion = f32[4,256,512]{2,1,0:T(8,128)} fusion(f32[4,256,512]{2,1,0:T(8,128)S(1)} %fusion.62, f32[4,512,256]{2,1,0:T(8,128)S(1)} %bitcast.318), kind=kOutput, calls=%fused_computation.72 | convolution fusion | flops 3225419776 | bytes 6291456 | tf_op jit(solution)/shard_map/mb,pkbc->pkmc/dot_general | solution.py:21
  314.8 34.9 %all-to-all-done.1 = f32[2,32,64,256]{3,2,0,1:T(8,128)} async-done(((f32[2,32,64,256]{3,2,0,1:T(8,128)}), f32[2,32,64,256]{3,2,0,1:T(8,128)}, u32[]{:S(2)}, u32[]{:S(2)}) %all-to-all-start.1) | async-done | bytes 4194336 | tf_op jit(solution)/shard_map/all_to_all | solution.py:43
  349.7 2.5 copy.84
  352.9 10.8 %fusion.67 = f32[4,256,512]{2,1,0:T(8,128)S(1)} fusion(f32[4,512,256]{2,1,0:T(8,128)S(1)} %bitcast.326), kind=kOutput, calls=%fused_computation.106 | convolution fusion | flops 3224895488 | bytes 4194304 | tf_op jit(solution)/shard_map/mb,pkbc->pkmc/dot_general | solution.py:21
  363.9 11.3 %fusion.69 = f32[4,256,512]{2,1,0:T(8,128)S(1)} fusion(f32[4,512,256]{2,1,0:T(8,128)S(1)} %bitcast.321), kind=kOutput, calls=%fused_computation.108 | convolution fusion | flops 3224895488 | bytes 4194304 | tf_op jit(solution)/shard_map/mb,pkbc->pkmc/dot_general | solution.py:21
  375.2 11.2 %convolution_subtract_fusion.1 = f32[4,256,512]{2,1,0:T(8,128)S(1)} fusion(f32[4,256,512]{2,1,0:T(8,128)S(1)} %fusion.67, f32[4,512,256]{2,1,0:T(8,128)S(1)} %bitcast.322), kind=kOutput, calls=%fused_computation.73 | convolution fusion | flops 3225419776 | bytes 6291456 | tf_op jit(solution)/shard_map/mb,pkbc->pkmc/dot_general | solution.py:21
  386.5 13.0 %fusion.11 = (f32[1,4,512,256]{2,3,1,0:T(8,128)}, f32[1,4,512,256]{2,3,1,0:T(8,128)}, f32[4,512,256]{1,2,0:T(8,128)S(1)}, f32[1,4,512,256]{2,3,1,0:T(8,128)S(1)}...) fusion(f32[4,256,512]{2,1,0:T(8,128)S(1)} %copy-done.5, f32[4,256,512]{2,1,0:T(8,128)S(1)} %convolution_subtract_fusion, ...), kind=kOutput, calls=%fused_computation.24 | convolution fusion | flops 3234856960 | bytes 27262976 | tf_op jit(solution)/shard_map/mb,pkbc->pkmc/dot_general | solution.py:21
  399.5 8.4 fusion.52
  407.9 8.6 fusion.65
  416.5 8.4 fusion.47
  424.9 8.8 %fusion.58 = f32[4,256,512]{2,1,0:T(8,128)S(1)} fusion(f32[4,512,256]{1,2,0:T(8,128)S(1)} %get-tuple-element.41), kind=kOutput, calls=%fused_computation.97 | convolution fusion | flops 3224895488 | bytes 4194304 | tf_op jit(solution)/shard_map/bm,pkmc->pkbc/dot_general | solution.py:21
  433.7 8.5 fusion.28
  442.2 8.7 fusion.31
  450.9 8.5 fusion.34
  459.4 9.3 %fusion.1 = (f32[1,4,512,256]{2,3,1,0:T(8,128)}, f32[1,4,512,256]{2,3,1,0:T(8,128)}, f32[1,4,512,256]{2,3,1,0:T(8,128)S(1)}, f32[1,4,512,256]{2,3,1,0:T(8,128)S(1)}) fusion(f32[4,256,512]{2,1,0:T(8,128)S(1)} %fusion.34, f32[4,512]{1,0:T(4,128)S(1)} %get-tuple-element.58, f32[4,512]{1,0:T(4,128)S(1)} %get-tuple-element.57, f32[4,256,512]{2,1,0:T(8,128)S(1)} %fusion.28, ...), kind=kOutput, calls=%fused_computation.8 | convolution fusion | flops 3231711232 | bytes 18890752 | tf_op jit(solution)/shard_map/bm,pkmc->pkbc/dot_general | solution.py:21
  468.7 2.5 pad_maximum_fusion.1
  471.2 5.5 copy.92
  476.6 97.3 %all_to_all.120 = f32[2,4,512,256]{3,1,0,2:T(4,128)S(1)} all-to-all(f32[2,4,512,256]{3,1,0,2:T(4,128)} %copy.92), channel_id=1, replica_groups=mesh['dp'=4,'seq'=8] {'seq'}, dimensions={2} | all-to-all | bytes 8388608 | tf_op jit(solution)/shard_map/all_to_all | solution.py:79
  577.1 2.7 copy.95
  581.7 4.3 copy.94
  586.0 2.9 reshape.263
  588.9 3.6 fusion.113
  595.9 51.6 %all_to_all.121 = f32[1,32,64,256]{3,2,0,1:T(8,128)S(1)} all-to-all(f32[1,32,64,256]{3,2,0,1:T(8,128)S(1)} %copy.96), channel_id=1, replica_groups=mesh['dp'=4,'seq'=8] {'seq'}, dimensions={1} | all-to-all | bytes 4194304 | tf_op jit(solution)/shard_map/all_to_all | solution.py:86
  649.0 7.9 convolution_bitcast_fusion
  657.1 10.3 %fusion.45 = f32[4,512,1024]{2,1,0:T(8,128)} fusion(f32[256,1024]{1,0:T(8,128)S(1)} %copy-done, f32[4,512,256]{2,1,0:T(8,128)} %param.6, f32[4,512,256]{2,1,0:T(8,128)S(1)} %bitcast.311), kind=kOutput, calls=%fused_computation.84 | convolution fusion | flops 6442975232 | bytes 13631488 | tf_op jit(solution)/shard_map/abc,co->abo/dot_general | solution.py:111
  667.4 4.7 pad_maximum_fusion.3
  672.1 5.5 copy.108
  677.6 113.7 %all_to_all.122 = f32[2,4,512,256]{3,1,0,2:T(4,128)S(1)} all-to-all(f32[2,4,512,256]{3,1,0,2:T(4,128)} %copy.108), channel_id=1, replica_groups=mesh['dp'=4,'seq'=8] {'seq'}, dimensions={2} | all-to-all | bytes 8388608 | tf_op jit(solution)/shard_map/all_to_all | solution.py:79
  794.3 2.7 copy.111
  797.0 3.0 reshape.271
  800.0 4.3 copy.110
  804.3 2.9 reshape.270
  807.3 3.9 fusion.109
  813.3 2.5 copy.112
  815.8 4.4 all-to-all-start.7
  820.2 5.0 maximum_multiply_fusion
  825.2 5.2 copy.115
  830.4 3.2 mul.571
  833.6 33.9 %all-to-all-done.7 = f32[1,32,64,256]{3,2,0,1:T(8,128)} async-done(((f32[1,32,64,256]{3,2,0,1:T(8,128)}), f32[1,32,64,256]{3,2,0,1:T(8,128)}, u32[]{:S(2)}, u32[]{:S(2)}) %all-to-all-start.7) | async-done | bytes 2097184 | tf_op jit(solution)/shard_map/all_to_all | solution.py:86
  867.5 3.1 copy.113
  870.6 2.3 copy.134
  (64 shorter events, 30.6 us)
Async XLA Ops:
  7.2 63.4 %copy-start = (f32[256,1024]{1,0:T(8,128)S(1)}, f32[256,1024]{1,0:T(8,128)}, u32[]{:S(2)}) copy-start(f32[256,1024]{1,0:T(8,128)} %param.9) | copy-start | bytes 3145732
  7.2 1.7 copy-start.11
  7.2 63.4 %all-gather.2.cloned.1.call-start = ((), (), s32[]{:S(2)}) async-start(), calls=%async_computation.10 | async-start | bytes 10485760 | tf_op jit(solution)/shard_map/all_gather | solution.py:92
  11.5 72.3 %all-to-all-start = ((f32[1,4,512,256]{3,1,0,2:T(4,128)}), f32[1,4,512,256]{3,1,0,2:T(4,128)}, u32[]{:S(2)}, u32[]{:S(2)}) async-start(f32[1,4,512,256]{3,1,0,2:T(4,128)} %bitcast.307), calls=%async_computation | async-start | bytes 4194304 | tf_op jit(solution)/shard_map/all_to_all | solution.py:33
  18.8 60.9 %copy-start.2 = (f32[4,512,256]{2,1,0:T(8,128)S(1)}, f32[4,512,256]{2,1,0:T(8,128)}, u32[]{:S(2)}) copy-start(f32[4,512,256]{2,1,0:T(8,128)} %param.6) | copy-start | bytes 6291460
  79.7 1.4 copy-start.1
  83.8 54.5 %all-to-all-start.4 = ((f32[1,4,512,256]{3,1,0,2:T(4,128)}), f32[1,4,512,256]{3,1,0,2:T(4,128)}, u32[]{:S(2)}, u32[]{:S(2)}) async-start(f32[1,4,512,256]{3,1,0,2:T(4,128)} %copy.98), calls=%async_computation.5 | async-start | bytes 4194304 | tf_op jit(solution)/shard_map/all_to_all | solution.py:33
  143.8 2.0 copy-start.8
  143.8 2.2 copy-start.9
  155.2 4.7 copy-start.10
  155.2 97.5 %all-to-all-start.5 = ((f32[2,32,64,256]{3,2,0,1:T(8,128)}), f32[2,32,64,256]{3,2,0,1:T(8,128)}, u32[]{:S(2)}, u32[]{:S(2)}) async-start(f32[2,32,64,256]{3,2,0,1:T(8,128)} %copy.100), calls=%async_computation.6 | async-start | bytes 8388608 | tf_op jit(solution)/shard_map/all_to_all | solution.py:43
  252.7 97.1 %all-to-all-start.1 = ((f32[2,32,64,256]{3,2,0,1:T(8,128)}), f32[2,32,64,256]{3,2,0,1:T(8,128)}, u32[]{:S(2)}, u32[]{:S(2)}) async-start(f32[2,32,64,256]{3,2,0,1:T(8,128)} %copy.83), calls=%async_computation.1 | async-start | bytes 8388608 | tf_op jit(solution)/shard_map/all_to_all | solution.py:43
  257.2 613.4 %all-reduce.2.cloned.1.call-start = ((), (), s32[]{:S(2)}) async-start(), calls=%async_computation.11 | async-start | bytes 2097152 | tf_op jit(solution)/shard_map/psum | solution.py:114
  375.2 11.3 %copy-start.5 = (f32[4,256,512]{2,1,0:T(8,128)S(1)}, f32[4,256,512]{2,1,0:T(8,128)}, u32[]{:S(2)}) copy-start(f32[4,256,512]{2,1,0:T(8,128)} %convolution_add_fusion) | copy-start | bytes 6291460
  375.2 11.3 %copy-start.6 = (f32[1,4,512,256]{2,3,1,0:T(8,128)S(1)}, f32[1,4,512,256]{2,3,1,0:T(8,128)}, u32[]{:S(2)}) copy-start(f32[1,4,512,256]{2,3,1,0:T(8,128)} %copy.126) | copy-start | bytes 6291460
  375.2 11.2 %copy-start.7 = (f32[1,4,512,256]{2,3,1,0:T(8,128)S(1)}, f32[1,4,512,256]{2,3,1,0:T(8,128)}, u32[]{:S(2)}) copy-start(f32[1,4,512,256]{2,3,1,0:T(8,128)} %copy.125) | copy-start | bytes 6291460
  592.5 55.1 %slice-start = ((s8[8388608]{0:T(1024)(128)(4,1)}), s8[4194304]{0:T(1024)(128)(4,1)S(1)}, s32[]{:S(2)}) async-start(s8[8388608]{0:T(1024)(128)(4,1)} %bitcast.308), calls=%async_computation.12 | async-start | bytes 8388608
  594.6 53.0 %slice-start.1 = ((s8[8388608]{0:T(1024)(128)(4,1)}), s8[4194304]{0:T(1024)(128)(4,1)S(1)}, s32[]{:S(2)}) async-start(s8[8388608]{0:T(1024)(128)(4,1)} %bitcast.308), calls=%async_computation.13 | async-start | bytes 8388608
  647.4 1.6 copy-start.3
  657.0 213.6 %reduce-scatter.2.cloned.1.call-start = ((), (), s32[]{:S(2)}) async-start(), calls=%async_computation.9 | async-start | bytes 10485760 | tf_op jit(solution)/shard_map/reduce_scatter | solution.py:112
  807.3 3.9 copy-start.4
  815.8 51.7 %all-to-all-start.7 = ((f32[1,32,64,256]{3,2,0,1:T(8,128)}), f32[1,32,64,256]{3,2,0,1:T(8,128)}, u32[]{:S(2)}, u32[]{:S(2)}) async-start(f32[1,32,64,256]{3,2,0,1:T(8,128)} %copy.112), calls=%async_computation.8 | async-start | bytes 4194304 | tf_op jit(solution)/shard_map/all_to_all | solution.py:86
Sparse Core Ops, SparseCore 0:
  9.6 60.9 all-gather.1
  657.1 99.4 all-reduce.1
  759.9 70.3 reduce-scatter.1
where the time goes:
time: 887 us; the launch traced here: 880 us
  blocking collectives  263 us (30%)
  waiting for transfers between devices  244 us (28%)
  matrix products  212 us (24%)
  local copies, waits for them, and re-layouts  101 us (11%)
  starting transfers between devices  26.9 us (3%)
  other arithmetic  18.3 us (2%)
  between operations  14.5 us (2%)
    all_to_all x2, blocking collectives, inverse(): lax.all_to_all(stacked, 'seq', split_axis=2, concat_axis=1, tiled=True)  211 us
    dot_general x24, matrix products, contract(): return jnp.einsum(form, matrix, field, precision=PRECISE)  185 us
    all_to_all x2, waiting for transfers between devices, forward(): lax.all_to_all(stacked, 'seq', split_axis=1, concat_axis=2, tiled=True)  121 us
    all_gather x1, waiting for transfers between devices, on_device(): cot_full = lax.all_gather(cotangent, 'dp', axis=2, tiled=True)  51.8 us
    all_to_all x1, blocking collectives, inverse(): lax.all_to_all(real_out, 'seq', split_axis=1, concat_axis=2, tiled=True)  51.6 us
    all_to_all x2, waiting for transfers between devices, forward(): lax.all_to_all(fields, 'seq', split_axis=2, concat_axis=1, tiled=True)  36.4 us
    all_to_all x1, waiting for transfers between devices, inverse(): lax.all_to_all(real_out, 'seq', split_axis=1, concat_axis=2, tiled=True)  33.9 us
    unnamed x33, local copies, waits for them, and re-layouts  19 us
  transfers between devices with their start and end apart: 8, of which 5 were waited for; matrix products, arithmetic and copies ran while one was open for 17% of the time, Pallas kernels for 0%

commit v1 on v0

v1 whole, which is shorter than its diff:
```python
import jax
import jax.numpy as jnp
import numpy as np
from jax import lax
from jax.sharding import PartitionSpec as P

PRECISE = lax.Precision.HIGH


def dft(n):
    index = np.arange(n, dtype=np.int64)
    angle = (index[:, None] * index[None, :] % n) * (2.0 * np.pi / n)
    return np.cos(angle).astype(np.float32), np.sin(angle).astype(np.float32)


def twiddle(n1, n2):
    index = np.arange(n1, dtype=np.int64)[:, None] * np.arange(n2, dtype=np.int64)[None, :]
    angle = (index % (n1 * n2)) * (2.0 * np.pi / (n1 * n2))
    shape = (n1, 1, n2)
    return (
        np.cos(angle).astype(np.float32).reshape(shape),
        np.sin(angle).astype(np.float32).reshape(shape),
    )


def contract(form, left, right):
    return jnp.einsum(form, left, right, precision=PRECISE)


def to_channels(field):
    devices = lax.axis_size("seq")
    rows, cols, channels = field.shape
    share = channels // devices
    blocks = field.reshape(rows, cols, devices, share).transpose(2, 0, 3, 1)
    moved = lax.all_to_all(blocks, "seq", split_axis=0, concat_axis=0, tiled=True)
    return moved.reshape(devices * rows, share, cols)


def to_rows(field):
    devices = lax.axis_size("seq")
    all_rows, share, cols = field.shape
    rows = all_rows // devices
    blocks = field.reshape(devices, rows, share, cols)
    moved = lax.all_to_all(blocks, "seq", split_axis=0, concat_axis=0, tiled=True)
    return moved.transpose(1, 3, 0, 2).reshape(rows, cols, devices * share)


def forward(field):
    n1, _, n2 = field.shape
    cos1, sin1 = dft(n1)
    cos2, sin2 = dft(n2)
    tcos, tsin = twiddle(n1, n2)
    re = contract("ka,acb->kcb", cos1, field)
    im = -contract("ka,acb->kcb", sin1, field)
    tre = re * tcos + im * tsin
    tim = im * tcos - re * tsin
    return (
        contract("kcb,bm->kcm", tre, cos2) + contract("kcb,bm->kcm", tim, sin2),
        contract("kcb,bm->kcm", tim, cos2) - contract("kcb,bm->kcm", tre, sin2),
    )


def inverse(re, im):
    n1, _, n2 = re.shape
    cos1, sin1 = dft(n1)
    cos2, sin2 = dft(n2)
    tcos, tsin = twiddle(n1, n2)
    hre = contract("kcm,mb->kcb", re, cos2) - contract("kcm,mb->kcb", im, sin2)
    him = contract("kcm,mb->kcb", im, cos2) + contract("kcm,mb->kcb", re, sin2)
    tre = hre * tcos - him * tsin
    tim = him * tcos + hre * tsin
    scale = np.float32(1.0 / (n1 * n2))
    return contract("ak,kcb->acb", cos1 * scale, tre) - contract("ak,kcb->acb", sin1 * scale, tim)


def on_device(signal, gate, cotangent, kernel, out_weight):
    sig = to_channels(signal)
    kern_re = to_channels(kernel[0])
    kern_im = to_channels(kernel[1])

    cot_full = lax.all_gather(cotangent, "dp", axis=2, tiled=True)
    gated_grad = contract("abo,co->abc", cot_full, out_weight)
    conv = to_channels(gated_grad * gate)

    sre, sim = forward(sig)
    mixed = to_rows(inverse(kern_re * sre - kern_im * sim, kern_re * sim + kern_im * sre))

    gre, gim = forward(conv)
    size = np.float32(1.0 / (gre.shape[0] * gre.shape[2]))
    kgrad_re = to_rows((sre * gre + sim * gim) * size)
    kgrad_im = to_rows((sre * gim - sim * gre) * size)
    input_grad = to_rows(inverse(kern_re * gre + kern_im * gim, kern_re * gim - kern_im * gre))

    gated = gate * mixed
    gate_grad = gated_grad * mixed
    out_term = contract("abc,co->abo", gated, out_weight)
    output = lax.psum_scatter(out_term, "dp", scatter_dimension=2, tiled=True)
    weight_grad = lax.psum(contract("abc,abo->co", gated, cot_full), "seq")
    return output, gate_grad, input_grad, jnp.stack([kgrad_re, kgrad_im]), weight_grad


def solution(mesh):
    grid = P("seq", None, "dp")
    spectrum = P(None, "seq", None, "dp")
    weight = P("dp", None)
    return jax.shard_map(
        on_device,
        mesh=mesh,
        in_specs=(grid, grid, grid, spectrum, weight),
        out_specs=(grid, grid, grid, spectrum, weight),
        check_vma=False,
    )
```

time: 887 us -> 531 us (0.60)
  blocking collectives: 263 us -> 116 us
  matrix products: 212 us -> 104 us
  local copies, waits for them, and re-layouts: 101 us -> 55 us
  waiting for transfers between devices: 244 us -> 201 us
  other arithmetic: 18.3 us -> 4.93 us
    all_to_all x3 -> x2, blocking collectives: 263 us -> 116 us  [to_rows(): lax.all_to_all(blocks, 'seq', split_axis=0, concat_axis=0, tiled=True)]
    dot_general x27, matrix products: 212 us -> 104 us  [contract(): return jnp.einsum(form, left, right, precision=PRECISE)]
    all_gather x1, waiting for transfers between devices: 51.8 us -> 0.02 us  [on_device(): cot_full = lax.all_gather(cotangent, 'dp', axis=2, tiled=True)]
    concatenate x4 -> x0, local copies, waits for them, and re-layouts: 19.8 us -> none  [the longest x2 11 us: inverse(): stacked = jnp.concatenate([turned_re, turned_im], axis=0)]
    slice x13 -> x1, local copies, waits for them, and re-layouts: 22.9 us -> 5.59 us  [on_device(): kern_re = to_channels(kernel[0])]
    another operation x5 -> x0, local copies, waits for them, and re-layouts: 12.8 us -> none
    all_to_all x8 -> x3, local copies, waits for them, and re-layouts: 18 us -> 5.39 us  [to_rows(): lax.all_to_all(blocks, 'seq', split_axis=0, concat_axis=0, tiled=True)]
    concatenate x4 -> x0, other arithmetic: 9.49 us -> none  [the longest x2 7.15 us: inverse(): stacked = jnp.concatenate([turned_re, turned_im], axis=0)]
  transfers between devices with their start and end apart: 8 -> 9, of which waited for: 5 -> 6; matrix products, arithmetic and copies ran while one was open for 17% -> 22% of each run, Pallas kernels for 0% -> 0%
where the time goes in v1:
time: 531 us; the launch traced here: 524 us
  waiting for transfers between devices  201 us (38%)
  blocking collectives  116 us (22%)
  matrix products  104 us (20%)
  local copies, waits for them, and re-layouts  55 us (10%)
  starting transfers between devices  29 us (5%)
  between operations  14.4 us (3%)
    all_to_all x4, waiting for transfers between devices, to_channels(): lax.all_to_all(blocks, 'seq', split_axis=0, concat_axis=0, tiled=True)  122 us
    all_to_all x2, blocking collectives, to_rows(): lax.all_to_all(blocks, 'seq', split_axis=0, concat_axis=0, tiled=True)  116 us
    dot_general x27, matrix products, contract(): return jnp.einsum(form, left, right, precision=PRECISE)  104 us
    all_to_all x2, waiting for transfers between devices, to_rows(): lax.all_to_all(blocks, 'seq', split_axis=0, concat_axis=0, tiled=True)  78.5 us
    unnamed x56, local copies, waits for them, and re-layouts  26.4 us
    all_to_all x4, starting transfers between devices, to_channels(): lax.all_to_all(blocks, 'seq', split_axis=0, concat_axis=0, tiled=True)  19.6 us
  transfers between devices with their start and end apart: 9, of which 6 were waited for; matrix products, arithmetic and copies ran while one was open for 22% of the time, Pallas kernels for 0%

profile of v1, /device:TPU:0, one launch (start us, length us, event | category | flops | bytes accessed | tf_op | source)
XLA Modules:
  0.0 523.8 jit_solution(4304977332335433247)
XLA Ops:
  7.9 1.9 copy.105
  9.8 1.5 copy.106
  11.4 7.3 %all-to-all-start.1 = ((f32[8,4,32,512]{3,2,1,0:T(8,128)}), f32[8,4,32,512]{3,2,1,0:T(8,128)S(1)}, u32[]{:S(2)}, u32[]{:S(2)}) async-start(f32[8,4,32,512]{3,2,1,0:T(8,128)} %copy.106), calls=%async_computation.1 | async-start | bytes 4194304 | tf_op jit(solution)/shard_map/all_to_all | solution.py:35
  18.7 5.6 %fusion.102 = (f32[1,4,512,256]{3,2,1,0:T(8,128)}, f32[1,4,512,256]{3,2,1,0:T(8,128)}) fusion(f32[2,4,512,256]{3,2,1,0:T(8,128)} %param.40), kind=kLoop, calls=%fused_computation.103 | loop fusion | bytes 8388608 | tf_op jit(solution)/shard_map/slice | solution.py:78
  24.3 3.1 copy.156
  27.3 3.2 copy.104
  30.5 36.4 %all-to-all-done.1 = f32[8,4,32,512]{3,2,1,0:T(8,128)S(1)} async-done(((f32[8,4,32,512]{3,2,1,0:T(8,128)}), f32[8,4,32,512]{3,2,1,0:T(8,128)S(1)}, u32[]{:S(2)}, u32[]{:S(2)}) %all-to-all-start.1) | async-done | bytes 2097184 | tf_op jit(solution)/shard_map/all_to_all | solution.py:35
  66.9 1.3 copy-done.9
  68.2 4.4 all-to-all-start
  72.6 1.9 copy.120
  74.6 9.1 %fusion.103 = (f32[4,512,256]{1,2,0:T(8,128)S(1)}, f32[4,512,256]{1,2,0:T(8,128)}) fusion(f32[4,512,256]{1,2,0:T(8,128)S(1)} %copy.120, f32[4,512,1024]{2,1,0:T(8,128)} %all-gather.2.cloned.1.call-done, f32[256,1024]{1,0:T(8,128)S(1)} %copy-done), kind=kOutput, calls=%fused_computation.104 | convolution fusion | flops 3221749760 | bytes 15728640 | tf_op jit(solution)/shard_map/abo,co->abc/dot_general | solution.py:27
  83.7 1.5 copy.219
  85.1 35.3 %all-to-all-done = f32[8,4,32,512]{3,2,1,0:T(8,128)} async-done(((f32[8,4,32,512]{3,2,1,0:T(8,128)}), f32[8,4,32,512]{3,2,1,0:T(8,128)}, u32[]{:S(2)}, u32[]{:S(2)}) %all-to-all-start) | async-done | bytes 2097184 | tf_op jit(solution)/shard_map/all_to_all | solution.py:35
  120.4 3.6 all-to-all-start.4
  124.0 2.9 copy.157
  126.9 3.4 copy.111
  130.3 3.4 fusion.26
  133.7 38.7 %all-to-all-done.4 = f32[8,4,32,512]{3,2,1,0:T(8,128)S(1)} async-done(((f32[8,4,32,512]{3,2,1,0:T(8,128)}), f32[8,4,32,512]{3,2,1,0:T(8,128)S(1)}, u32[]{:S(2)}, u32[]{:S(2)}) %all-to-all-start.4) | async-done | bytes 2097184 | tf_op jit(solution)/shard_map/all_to_all | solution.py:35
  172.4 4.4 all-to-all-start.2
  177.1 3.7 fusion.28
  180.8 2.3 fusion.22
  183.2 4.8 fusion
  188.1 2.7 fusion.46
  190.8 3.1 fusion.48
  193.9 4.0 fusion.54
  197.9 2.7 fusion.56
  200.7 4.1 fusion.72
  204.7 4.1 fusion.75
  208.8 4.2 fusion.66
  213.1 11.6 %all-to-all-done.2 = f32[8,4,32,512]{3,2,1,0:T(8,128)} async-done(((f32[8,4,32,512]{3,2,1,0:T(8,128)}), f32[8,4,32,512]{3,2,1,0:T(8,128)}, u32[]{:S(2)}, u32[]{:S(2)}) %all-to-all-start.2) | async-done | bytes 2097184 | tf_op jit(solution)/shard_map/all_to_all | solution.py:35
  224.6 11.7 %add_multiply_fusion = (f32[32,32,512]{2,1,0:T(8,128)}, f32[32,32,512]{2,1,0:T(8,128)}, f32[32,32,512]{2,1,0:T(8,128)}, f32[32,32,512]{2,1,0:T(8,128)}, f32[32,3...) fusion(f32[32,32,512]{2,1,0:T(8,128)} %fusion.75, f32[32,32,512]{2,1,0:T(8,128)} %fusion.66, f32[32,32,512]{2,1,0:T(8,128)} %fusion.72, ...), kind=kOutput, calls=%fused_computation.21 | convolution fusion | flops 1621622784 | bytes 28311552 | tf_op jit(solution)/shard_map/kcb,bm->kcm/dot_general | solution.py:27
  236.4 2.6 fusion.38
  239.0 2.6 fusion.40
  241.7 2.6 fusion.81
  244.3 2.6 fusion.78
  247.0 1.8 fusion.14
  248.8 2.9 subtract_bitcast_fusion.1
  251.7 2.8 reshape.50
  254.5 2.0 copy.118
  256.6 52.1 %all_to_all.40 = f32[8,4,32,512]{3,1,2,0:T(4,128)S(1)} all-to-all(f32[8,4,32,512]{3,1,2,0:T(4,128)S(1)} %copy.118), channel_id=1, replica_groups=mesh['dp'=4,'seq'=8] {'seq'}, dimensions={0} | all-to-all | bytes 4194304 | tf_op jit(solution)/shard_map/all_to_all | solution.py:44
  309.3 0.9 copy-done.6
  310.9 2.1 bitcast_multiply_fusion.2
  313.0 1.3 copy-done.11
  314.3 5.4 %convolution_bitcast_fusion = f32[256,1024]{1,0:T(8,128)} fusion(f32[4,512,256]{1,2,0:T(8,128)S(1)} %get-tuple-element.37, f32[4,512,1024]{2,1,0:T(8,128)S(1)} %bitcast.114), kind=kOutput, calls=%fused_computation.90 | convolution fusion | flops 3221225472 | bytes 11534336 | tf_op jit(solution)/shard_map/abc,abo->co/dot_general | solution.py:27
  319.7 7.4 %fusion.92 = f32[4,512,1024]{2,1,0:T(8,128)} fusion(f32[4,512,256]{1,2,0:T(8,128)} %copy-done.11, f32[256,1024]{1,0:T(8,128)S(1)} %copy-done), kind=kOutput, calls=%fused_computation.93 | convolution fusion | flops 3221225472 | bytes 11534336 | tf_op jit(solution)/shard_map/abc,co->abo/dot_general | solution.py:27
  327.1 63.5 %all_to_all.41 = f32[8,4,32,512]{3,2,1,0:T(8,128)} all-to-all(f32[8,4,32,512]{3,2,1,0:T(8,128)} %bitcast.120), channel_id=1, replica_groups=mesh['dp'=4,'seq'=8] {'seq'}, dimensions={0} | all-to-all | bytes 4194304 | tf_op jit(solution)/shard_map/all_to_all | solution.py:44
  390.6 4.6 all-to-all-start.6
  395.2 4.4 fusion.30
  399.7 2.7 fusion.32
  402.4 2.7 fusion.87
  405.1 2.7 fusion.84
  407.8 1.6 fusion.6
  409.4 1.6 subtract_bitcast_fusion
  410.9 2.5 copy.155
  413.5 40.3 %all-to-all-done.6 = f32[8,4,32,512]{3,2,1,0:T(8,128)} async-done(((f32[8,4,32,512]{3,2,1,0:T(8,128)}), f32[8,4,32,512]{3,2,1,0:T(8,128)}, u32[]{:S(2)}, u32[]{:S(2)}) %all-to-all-start.6) | async-done | bytes 2097184 | tf_op jit(solution)/shard_map/all_to_all | solution.py:44
  453.7 4.5 all-to-all-start.5
  458.5 1.9 copy.135
  460.4 2.8 pad_maximum_fusion
  463.2 5.2 copy.139
  468.5 38.3 %all-to-all-done.5 = f32[8,4,32,512]{3,2,1,0:T(8,128)} async-done(((f32[8,4,32,512]{3,2,1,0:T(8,128)}), f32[8,4,32,512]{3,2,1,0:T(8,128)}, u32[]{:S(2)}, u32[]{:S(2)}) %all-to-all-start.5) | async-done | bytes 2097184 | tf_op jit(solution)/shard_map/all_to_all | solution.py:44
  506.7 3.2 copy.134
  509.9 3.0 copy.138
  512.9 1.8 copy.137
  514.8 2.3 copy.221
  (57 shorter events, 2.7 us)
Async XLA Ops:
  7.2 67.4 %copy-start = (f32[256,1024]{1,0:T(8,128)S(1)}, f32[256,1024]{1,0:T(8,128)}, u32[]{:S(2)}) copy-start(f32[256,1024]{1,0:T(8,128)} %param.41) | copy-start | bytes 3145732
  7.2 67.4 %all-gather.2.cloned.1.call-start = ((), (), s32[]{:S(2)}) async-start(), calls=%async_computation.10 | async-start | bytes 10485760 | tf_op jit(solution)/shard_map/all_gather | solution.py:81
  11.4 55.5 %all-to-all-start.1 = ((f32[8,4,32,512]{3,2,1,0:T(8,128)}), f32[8,4,32,512]{3,2,1,0:T(8,128)S(1)}, u32[]{:S(2)}, u32[]{:S(2)}) async-start(f32[8,4,32,512]{3,2,1,0:T(8,128)} %copy.106), calls=%async_computation.1 | async-start | bytes 4194304 | tf_op jit(solution)/shard_map/all_to_all | solution.py:35
  66.9 1.3 copy-start.9
  68.2 52.2 %all-to-all-start = ((f32[8,4,32,512]{3,2,1,0:T(8,128)}), f32[8,4,32,512]{3,2,1,0:T(8,128)}, u32[]{:S(2)}, u32[]{:S(2)}) async-start(f32[8,4,32,512]{3,2,1,0:T(8,128)} %copy.104), calls=%async_computation | async-start | bytes 4194304 | tf_op jit(solution)/shard_map/all_to_all | solution.py:35
  74.5 9.1 %copy-start.5 = (f32[4,512,256]{1,2,0:T(8,128)}, f32[4,512,256]{1,2,0:T(8,128)S(1)}, u32[]{:S(2)}) copy-start(f32[4,512,256]{1,2,0:T(8,128)S(1)} %copy.120) | copy-start | bytes 6291460
  120.4 52.0 %all-to-all-start.4 = ((f32[8,4,32,512]{3,2,1,0:T(8,128)}), f32[8,4,32,512]{3,2,1,0:T(8,128)S(1)}, u32[]{:S(2)}, u32[]{:S(2)}) async-start(f32[8,4,32,512]{3,2,1,0:T(8,128)} %bitcast.123), calls=%async_computation.5 | async-start | bytes 4194304 | tf_op jit(solution)/shard_map/all_to_all | solution.py:35
  126.9 3.4 copy-start.10
  126.9 3.4 copy-start.20
  133.7 43.3 %copy-start.21 = (f32[32,32,1]{1,0,2:T(8,128)S(1)}, f32[32,32,1]{1,0,2:T(8,128)}, u32[]{:S(2)}) copy-start(f32[32,32,1]{1,0,2:T(8,128)} %constant.32) | copy-start | bytes 12292
  172.4 8.4 %copy-start.8 = (f32[8,4,32,512]{3,2,1,0:T(8,128)}, f32[8,4,32,512]{3,2,1,0:T(8,128)S(1)}, u32[]{:S(2)}) copy-start(f32[8,4,32,512]{3,2,1,0:T(8,128)S(1)} %all-to-all-done.4) | copy-start | bytes 6291460
  172.4 52.2 %all-to-all-start.2 = ((f32[8,4,32,512]{3,2,1,0:T(8,128)}), f32[8,4,32,512]{3,2,1,0:T(8,128)}, u32[]{:S(2)}, u32[]{:S(2)}) async-start(f32[8,4,32,512]{3,2,1,0:T(8,128)} %copy.111), calls=%async_computation.2 | async-start | bytes 4194304 | tf_op jit(solution)/shard_map/all_to_all | solution.py:35
  176.8 337.9 %all-reduce.2.cloned.1.call-start = ((), (), s32[]{:S(2)}) async-start(), calls=%async_computation.11 | async-start | bytes 2097152 | tf_op jit(solution)/shard_map/psum | solution.py:98
  180.8 2.4 copy-start.14
  180.8 2.4 copy-start.16
  180.8 2.4 copy-start.17
  183.2 4.8 copy-start.2
  188.0 20.8 %copy-start.4 = (f32[32,32,512]{2,0,1:T(8,128)}, f32[32,32,512]{2,0,1:T(8,128)S(1)}, u32[]{:S(2)}) copy-start(f32[32,32,512]{2,0,1:T(8,128)S(1)} %get-tuple-element.39) | copy-start | bytes 6291460
  188.0 2.7 copy-start.1
  244.3 2.7 copy-start.19
  247.0 1.8 copy-start.18
  256.6 57.7 %slice-start = ((s8[8388608]{0:T(1024)(128)(4,1)}), s8[4194304]{0:T(1024)(128)(4,1)S(1)}, s32[]{:S(2)}) async-start(s8[8388608]{0:T(1024)(128)(4,1)} %bitcast.113), calls=%async_computation.12 | async-start | bytes 8388608
  308.6 1.6 copy-start.6
  308.6 2.2 copy-start.12
  310.9 3.5 slice-start.1
  313.0 1.3 copy-start.11
  319.7 195.1 %reduce-scatter.2.cloned.1.call-start = ((), (), s32[]{:S(2)}) async-start(), calls=%async_computation.9 | async-start | bytes 10485760 | tf_op jit(solution)/shard_map/reduce_scatter | solution.py:97
  390.6 63.1 %all-to-all-start.6 = ((f32[8,4,32,512]{3,2,1,0:T(8,128)}), f32[8,4,32,512]{3,2,1,0:T(8,128)}, u32[]{:S(2)}, u32[]{:S(2)}) async-start(f32[8,4,32,512]{3,2,1,0:T(8,128)} %bitcast.119), calls=%async_computation.7 | async-start | bytes 4194304 | tf_op jit(solution)/shard_map/all_to_all | solution.py:44
  395.2 4.4 copy-start.7
  399.6 2.7 copy-start.3
  453.7 4.5 copy-start.15
  453.7 53.0 %all-to-all-start.5 = ((f32[8,4,32,512]{3,2,1,0:T(8,128)}), f32[8,4,32,512]{3,2,1,0:T(8,128)}, u32[]{:S(2)}, u32[]{:S(2)}) async-start(f32[8,4,32,512]{3,2,1,0:T(8,128)} %bitcast.122), calls=%async_computation.6 | async-start | bytes 4194304 | tf_op jit(solution)/shard_map/all_to_all | solution.py:44
  509.9 3.0 copy-start.13
Sparse Core Ops, SparseCore 0:
  9.6 60.9 all-gather.1
  319.8 103.1 all-reduce.1
  426.4 81.8 reduce-scatter.1
